TPU v7x, 128 devices: a whole 4x4x4 slice. The times are simulated.
128 devices in a mesh: str: 16 (over x_lo, y, core), crs: 8 (over x_hi, z).
Axes of the slice: x: 4 (x_hi: 2, x_lo: 2; x = x_hi * 2 + x_lo), y: 4, z: 4, core: 2. Of those that a mesh axis runs over, the one named last changes fastest.
Arguments:
- voltage: float32 [4, 512, 16384], P(None, 'str', 'crs'), may hold values from -4 to 0.5
- photocurrent: float32 [4, 512, 16384], P(None, 'str', 'crs'), may hold values from 0.1 to 10
- shunt: float32 [512, 16384], P('str', 'crs'), may hold values from 0.02 to 0.5
- series: float32 [512, 16384], P('str', 'crs'), may hold values from 0.5 to 2
- pattern: int32 [512, 128], P('str', 'crs'), may hold values from 0 to 3
- diode_mask: int32 [512, 128], P('str', 'crs'), may hold values 0 or 1
- aggregate: int32 [512, 128], P('str', 'crs'), may hold values from 0 to 4095, as said below
- coarse_inverse: float32 [4096, 4096], P('crs'), as said below
Outputs:
- newton_step: float32 [4, 512, 16384], P(None, 'str', 'crs')
- residual: float32 [4, 512, 16384], P(None, 'str', 'crs')
Inputs may be any that keep to these rules, and one draw needn't show every extreme that they name: `aggregate`: every value appears. coarse_inverse is symmetric positive definite.
All inputs are finite; a program needn't handle non-finite values. No bound on the sum of `diode_mask` on one device may be relied on, other than what follows from the above.
Results may differ from a plain program's by a relative error of at most 0.0003.
Values sent between devices are 32-bit elements; how exact they have to be, the bound alone decides.
A program may use at most 64 MiB of HBM per device.

v0:
```python
import jax
import jax.numpy as jnp
from jax import lax
from jax.sharding import PartitionSpec as P

ITERS = 3
LEVELS = (0.25, 0.5, 1.0, 2.0)
DIODE_SAT = 0.5


def with_halo(block, sides, width, periodic):
    for axis, dim in sides:
        count = lax.axis_size(axis)
        forward = [(i, i + 1) for i in range(count - 1)]
        if periodic:
            forward.append((count - 1, 0))
        backward = [(target, source) for source, target in forward]
        low = lax.ppermute(
            lax.slice_in_dim(block, block.shape[dim] - width, None, axis=dim), axis, forward
        )
        high = lax.ppermute(lax.slice_in_dim(block, 0, width, axis=dim), axis, backward)
        block = jnp.concatenate([low, block, high], axis=dim)
    return block


def widen(blocks):
    shape = blocks.shape
    spread = jnp.broadcast_to(blocks[..., None], shape + (128,))
    return spread.reshape(shape[:-1] + (shape[-1] * 128,))


def cross_levels(pattern):
    total = jnp.zeros(pattern.shape, jnp.float32)
    for number in range(4):
        total = total + jnp.where(pattern == number, jnp.float32(LEVELS[number]), jnp.float32(0.0))
    return total


def neighbours(field):
    along = with_halo(field, (("str", 1),), 1, True)
    across = with_halo(field, (("crs", 2),), 1, False)
    return (along[:, 2:], along[:, :-2], across[:, :, 2:], across[:, :, :-2])


def shards(voltage, photocurrent, shunt, series, pattern, diode_mask, aggregate, coarse_inverse):
    points = voltage.shape[0]
    rows_here = voltage.shape[1]
    local_block_list = voltage.shape[2] // 128
    coarse_count = coarse_inverse.shape[1]
    cross_level = widen(cross_levels(pattern))
    diode_area = widen(diode_mask.astype(jnp.float32))
    flat_groups = aggregate.reshape(-1)
    stacked = jnp.concatenate([voltage, cross_level[None], series[None]], axis=0)
    below, above, right_cells, left_cells = neighbours(stacked)
    right_link = jnp.minimum(cross_level, right_cells[points])
    left_link = jnp.minimum(cross_level, left_cells[points])
    up_link = above[points + 1]
    diode_derivative = DIODE_SAT * diode_area * jnp.exp(voltage)
    imbalance = (
        shunt * voltage
        + series * (voltage - below[:points])
        + up_link * (voltage - above[:points])
        + right_link * (voltage - right_cells[:points])
        + left_link * (voltage - left_cells[:points])
        + diode_derivative
        - DIODE_SAT * diode_area
        - photocurrent
    )
    diagonal = shunt + diode_derivative + series + up_link + right_link + left_link

    def restrict(remainder):
        block_sums = remainder.reshape(points, rows_here * local_block_list, 128).sum(axis=-1)
        return jax.ops.segment_sum(block_sums.T, flat_groups, num_segments=coarse_count).T

    def interpolate_upward(correction):
        picked = jnp.take(correction, flat_groups, axis=1)
        return widen(picked.reshape(points, rows_here, local_block_list))

    def coarse_solve(incomplete_value):
        product = None
        total = lax.psum(incomplete_value, ("str", "crs"))
        row_share = lax.dot_general(
            total, coarse_inverse, (((1,), (1,)), ((), ())), precision=lax.Precision.HIGHEST
        )
        correction = lax.all_gather(row_share, "crs", axis=1, tiled=True)
        return (correction, product)

    def precondition(remainder):
        resident_portion = remainder / diagonal
        incomplete_value = restrict(remainder)
        correction, product = coarse_solve(incomplete_value)
        smoothed = resident_portion + interpolate_upward(correction)
        product = lax.psum(jnp.sum(remainder * smoothed, axis=(1, 2)), ("str", "crs"))
        return (smoothed, product)

    remainder = -imbalance
    newton_step = jnp.zeros_like(voltage)
    smoothed, product = precondition(remainder)
    direction = smoothed
    for turn in range(ITERS):
        operate_below, operate_above, operate_right_cells, operate_left_cells = neighbours(
            direction
        )
        image = (
            diagonal * direction
            - series * operate_below
            - up_link * operate_above
            - right_link * operate_right_cells
            - left_link * operate_left_cells
        )
        curvature = lax.psum(jnp.sum(direction * image, axis=(1, 2)), ("str", "crs"))
        alpha = (product / curvature)[:, None, None]
        newton_step = newton_step + alpha * direction
        remainder = remainder - alpha * image
        if turn + 1 < ITERS:
            smoothed, fresh = precondition(remainder)
            ratio = (fresh / product)[:, None, None]
            direction = smoothed + ratio * direction
            product = fresh
    return (newton_step, remainder)


def solution(mesh):
    placed = (
        P(None, "str", "crs"),
        P(None, "str", "crs"),
        P("str", "crs"),
        P("str", "crs"),
        P("str", "crs"),
        P("str", "crs"),
        P("str", "crs"),
        P("crs", None),
    )
    return jax.shard_map(
        shards,
        mesh=mesh,
        in_specs=placed,
        out_specs=(P(None, "str", "crs"), P(None, "str", "crs")),
        check_vma=False,
    )
```

profile of v0, /device:TPU:1, one launch (start us, length us, event | category | flops | bytes accessed | tf_op | source)
XLA Modules:
  0.0 1062.8 jit_solution(3380685636923150555)
XLA Ops:
  13.7 4.2 collective-permute-start.3
  20.6 2.9 fusion.30
  26.5 3.8 scatter_custom_fusion
  30.4 158.7 %all-reduce.5.cloned.1.call-done = f32[4,4096]{0,1:T(8,128)} async-done(((f32[4,4096]{0,1:T(8,128)}), f32[4,4096]{0,1:T(8,128)}) %all-reduce.5.cloned.1.call-update) | async-done | bytes 65552 | tf_op jit(solution)/shard_map/psum | solution.py:81
  189.0 10.9 %fusion.54 = f32[4,512]{1,0:T(4,128)S(1)} fusion(f32[4,4096]{0,1:T(8,128)} %all-reduce.5.cloned.1.call-done, f32[512,4096]{1,0:T(8,128)} %param.17), kind=kOutput, calls=%fused_computation.118 | convolution fusion | flops 100663296 | bytes 8462336 | tf_op jit(solution)/shard_map/dot_general | solution.py:82
  199.9 28.1 %all_gather.9 = f32[4,4096]{1,0:T(4,128)S(1)} all-gather(f32[4,512]{1,0:T(4,128)S(1)} %fusion.54), channel_id=1, replica_groups=mesh['str'=16,'crs'=8] {'crs'}, dimensions={1}, use_global_device_ids=true | all-gather | bytes 73728 | tf_op jit(solution)/shard_map/all_gather | solution.py:85
  233.2 2.6 divide_add_fusion.2
  235.8 7.2 collective-permute-start.4
  245.6 4.0 collective-permute-start.7
  252.5 69.2 %all-reduce = (f32[4]{0:T(128)}, f32[4]{0:T(128)}) all-reduce(f32[4]{0:T(128)S(1)} %get-tuple-element.4, f32[4]{0:T(128)S(1)} %get-tuple-element.3), channel_id=1, replica_groups=mesh['str'=16,'crs'=8] {'str','crs'}, use_global_device_ids=true, to_apply=%region_4.6 | all-reduce | flops 8 | bytes 64 | tf_op jit(solution)/shard_map/psum | solution.py:93
  322.4 2.8 multiply_subtract_fusion.2
  327.1 3.8 scatter_custom_fusion.1
  331.1 147.5 %all-reduce.7.cloned.1.call-done = f32[4,4096]{0,1:T(8,128)} async-done(((f32[4,4096]{0,1:T(8,128)}), f32[4,4096]{0,1:T(8,128)}) %all-reduce.7.cloned.1.call-update) | async-done | bytes 65552 | tf_op jit(solution)/shard_map/psum | solution.py:81
  478.6 10.9 %fusion.55 = f32[4,512]{1,0:T(4,128)S(1)} fusion(f32[4,4096]{0,1:T(8,128)} %all-reduce.7.cloned.1.call-done, f32[512,4096]{1,0:T(8,128)} %param.17), kind=kOutput, calls=%fused_computation.119 | convolution fusion | flops 100663296 | bytes 8462336 | tf_op jit(solution)/shard_map/dot_general | solution.py:82
  489.4 27.8 %all_gather.10 = f32[4,4096]{1,0:T(4,128)S(1)} all-gather(f32[4,512]{1,0:T(4,128)S(1)} %fusion.55), channel_id=1, replica_groups=mesh['str'=16,'crs'=8] {'crs'}, dimensions={1}, use_global_device_ids=true | all-gather | bytes 73728 | tf_op jit(solution)/shard_map/all_gather | solution.py:85
  519.2 3.3 gather_fusion.1
  526.9 2.4 reshape.57
  530.8 70.0 %psum.67 = f32[4]{0:T(128)S(1)} all-reduce(f32[4]{0:T(128)S(1)} %multiply_reduce_fusion.3), channel_id=1, replica_groups=mesh['str'=16,'crs'=8] {'str','crs'}, use_global_device_ids=true, to_apply=%region_11.13 | all-reduce | flops 4 | bytes 32 | tf_op jit(solution)/shard_map/psum | solution.py:93
  606.0 4.0 collective-permute-start.11
  613.3 71.4 %psum.68 = f32[4]{0:T(128)} all-reduce(f32[4]{0:T(128)S(1)} %multiply_reduce_fusion.2), channel_id=1, replica_groups=mesh['str'=16,'crs'=8] {'str','crs'}, use_global_device_ids=true, to_apply=%region_13.15 | all-reduce | flops 4 | bytes 32 | tf_op jit(solution)/shard_map/psum | solution.py:111
  685.4 3.1 multiply_subtract_fusion.1
  688.5 2.4 reshape.58
  693.3 4.1 scatter_custom_fusion.2
  697.3 147.4 %all-reduce.9.cloned.1.call-done = f32[4,4096]{0,1:T(8,128)} async-done(((f32[4,4096]{0,1:T(8,128)}), f32[4,4096]{0,1:T(8,128)}) %all-reduce.9.cloned.1.call-update) | async-done | bytes 65552 | tf_op jit(solution)/shard_map/psum | solution.py:81
  844.8 10.9 %fusion.56 = f32[4,512]{1,0:T(4,128)S(1)} fusion(f32[4,4096]{0,1:T(8,128)} %all-reduce.9.cloned.1.call-done, f32[512,4096]{1,0:T(8,128)} %param.17), kind=kOutput, calls=%fused_computation.120 | convolution fusion | flops 100663296 | bytes 8462336 | tf_op jit(solution)/shard_map/dot_general | solution.py:82
  855.6 27.8 %all_gather.11 = f32[4,4096]{1,0:T(4,128)S(1)} all-gather(f32[4,512]{1,0:T(4,128)S(1)} %fusion.56), channel_id=1, replica_groups=mesh['str'=16,'crs'=8] {'crs'}, dimensions={1}, use_global_device_ids=true | all-gather | bytes 73728 | tf_op jit(solution)/shard_map/all_gather | solution.py:85
  885.4 3.2 gather_fusion.2
  893.0 2.4 reshape.59
  897.2 70.1 %psum.70 = f32[4]{0:T(128)S(1)} all-reduce(f32[4]{0:T(128)S(1)} %multiply_reduce_fusion.1), channel_id=1, replica_groups=mesh['str'=16,'crs'=8] {'str','crs'}, use_global_device_ids=true, to_apply=%region_18.20 | all-reduce | flops 4 | bytes 32 | tf_op jit(solution)/shard_map/psum | solution.py:93
  972.6 4.0 collective-permute-start.15
  979.9 71.0 %psum.71 = f32[4]{0:T(128)} all-reduce(f32[4]{0:T(128)S(1)} %multiply_reduce_fusion), channel_id=1, replica_groups=mesh['str'=16,'crs'=8] {'str','crs'}, use_global_device_ids=true, to_apply=%region_20.22 | all-reduce | flops 4 | bytes 32 | tf_op jit(solution)/shard_map/psum | solution.py:111
  1051.6 2.7 multiply_add_fusion
  (176 shorter events, 64.1 us)
Async XLA Ops:
  7.2 181.9 %all-reduce.5.cloned.1.call-start = ((), (), s32[]{:S(2)}) async-start(), calls=%async_computation | async-start | bytes 4194304 | tf_op jit(solution)/shard_map/psum | solution.py:81
  9.5 10.3 collective-permute-start
  11.0 8.6 collective-permute-start.1
  12.4 7.1 collective-permute-start.2
  13.7 5.8 collective-permute-start.3
  30.3 448.3 %all-reduce.7.cloned.1.call-start = ((), (), s32[]{:S(2)}) async-start(), calls=%async_computation.1 | async-start | bytes 4194304 | tf_op jit(solution)/shard_map/psum | solution.py:81
  199.9 30.4 %copy-start.36 = (pred[512]{0:T(512)(128)(4,1)S(1)}, pred[512]{0:T(512)(128)(4,1)}, u32[]{:S(2)}) copy-start(pred[512]{0:T(512)(128)(4,1)} %compare_and_fusion) | copy-start | bytes 1540
  233.2 18.4 %copy-start.4 = (f32[4,32,2048]{2,1,0:T(8,128)S(1)}, f32[4,32,2048]{2,1,0:T(8,128)}, u32[]{:S(2)}) copy-start(f32[4,32,2048]{2,1,0:T(8,128)} %copy-done.3) | copy-start | bytes 3145732
  233.2 18.4 %copy-start.8 = (f32[32,2048]{1,0:T(8,128)S(1)}, f32[32,2048]{1,0:T(8,128)}, u32[]{:S(2)}) copy-start(f32[32,2048]{1,0:T(8,128)} %copy-done.7) | copy-start | bytes 786436
  233.2 18.4 %copy-start.13 = (f32[32,2048]{1,0:T(8,128)S(1)}, f32[32,2048]{1,0:T(8,128)}, u32[]{:S(2)}) copy-start(f32[32,2048]{1,0:T(8,128)} %copy-done.12) | copy-start | bytes 786436
  233.2 18.4 %copy-start.18 = (f32[32,2048]{1,0:T(8,128)S(1)}, f32[32,2048]{1,0:T(8,128)}, u32[]{:S(2)}) copy-start(f32[32,2048]{1,0:T(8,128)} %copy-done.17) | copy-start | bytes 786436
  235.8 15.7 %collective-permute-start.4 = (f32[4,1,2048]{2,1,0:T(1,128)S(1)}, f32[4,1,2048]{2,1,0:T(1,128)S(1)}, u32[]{:S(2)}, u32[]{:S(2)}) collective-permute-start(f32[4,1,2048]{2,1,0:T(1,128)S(1)} %get-tuple-element.24), channel_id=1, source_target_pairs={{8,0},{16,8},{24,16},{32,24},{40,32},{48,40},{56,48},{64,56},{72,6... | collective-permute-start | bytes 98312 | tf_op jit(solution)/shard_map/ppermute | solution.py:21
  243.0 8.6 collective-permute-start.5
  244.3 5.4 collective-permute-start.6
  245.6 5.9 collective-permute-start.7
  251.6 70.8 %copy-start.5 = (f32[4,32,2048]{2,1,0:T(8,128)S(1)}, f32[4,32,2048]{2,1,0:T(8,128)}, u32[]{:S(2)}) copy-start(f32[4,32,2048]{2,1,0:T(8,128)} %copy-done.3) | copy-start | bytes 3145732
  330.9 513.9 %all-reduce.9.cloned.1.call-start = ((), (), s32[]{:S(2)}) async-start(), calls=%async_computation.2 | async-start | bytes 4194304 | tf_op jit(solution)/shard_map/psum | solution.py:81
  529.3 71.5 %copy-start.42 = (f32[4]{0:T(128)S(1)}, f32[4]{0:T(128)}, u32[]{:S(2)}) copy-start(f32[4]{0:T(128)} %get-tuple-element.5) | copy-start | bytes 52
  600.8 11.7 %copy-start.9 = (f32[32,2048]{1,0:T(8,128)S(1)}, f32[32,2048]{1,0:T(8,128)}, u32[]{:S(2)}) copy-start(f32[32,2048]{1,0:T(8,128)} %copy-done.7) | copy-start | bytes 786436
  600.8 11.7 %copy-start.14 = (f32[32,2048]{1,0:T(8,128)S(1)}, f32[32,2048]{1,0:T(8,128)}, u32[]{:S(2)}) copy-start(f32[32,2048]{1,0:T(8,128)} %copy-done.12) | copy-start | bytes 786436
  602.8 8.5 collective-permute-start.8
  604.0 7.3 collective-permute-start.9
  604.7 5.7 collective-permute-start.10
  606.0 5.3 collective-permute-start.11
  895.4 72.0 %copy-start.41 = (f32[4]{0:T(128)S(1)}, f32[4]{0:T(128)}, u32[]{:S(2)}) copy-start(f32[4]{0:T(128)} %copy-done.40) | copy-start | bytes 52
  967.4 11.7 %copy-start.10 = (f32[32,2048]{1,0:T(8,128)S(1)}, f32[32,2048]{1,0:T(8,128)}, u32[]{:S(2)}) copy-start(f32[32,2048]{1,0:T(8,128)} %copy-done.7) | copy-start | bytes 786436
  967.4 11.7 %copy-start.15 = (f32[32,2048]{1,0:T(8,128)S(1)}, f32[32,2048]{1,0:T(8,128)}, u32[]{:S(2)}) copy-start(f32[32,2048]{1,0:T(8,128)} %copy-done.12) | copy-start | bytes 786436
  967.4 11.7 %copy-start.20 = (f32[32,2048]{1,0:T(8,128)S(1)}, f32[32,2048]{1,0:T(8,128)}, u32[]{:S(2)}) copy-start(f32[32,2048]{1,0:T(8,128)} %copy-done.17) | copy-start | bytes 786436
  969.4 8.5 collective-permute-start.12
  970.5 7.3 collective-permute-start.13
  971.3 5.7 collective-permute-start.14
  972.6 5.3 collective-permute-start.15
  (30 other events, 110.5 us)
Sparse Core Ops, SparseCore 0:
  30.4 158.5 all-reduce.4
  331.0 147.5 all-reduce.6
  697.5 147.2 all-reduce.8
where the time goes:
time: 1070 us; the launch traced here: 1060 us
  waiting for transfers between devices  458 us (43%)
  blocking collectives  435 us (41%)
  other arithmetic  50.6 us (5%)
  starting transfers between devices  36.5 us (3%)
  local copies, waits for them, and re-layouts  35 us (3%)
  matrix products  32.6 us (3%)
  between operations  14.5 us (1%)
    psum x3, waiting for transfers between devices, coarse_solve(): total = lax.psum(incomplete_value, ('str', 'crs'))  454 us
    psum x3, blocking collectives, precondition(): lax.psum(jnp.sum(remainder * smoothed, axis=(1, 2)), ('str', 'crs'))  209 us
    psum x2, blocking collectives, shards(): lax.psum(jnp.sum(direction * image, axis=(1, 2)), ('str', 'crs'))  142 us
    all_gather x3, blocking collectives, coarse_solve(): correction = lax.all_gather(row_share, 'crs', axis=1, tiled=True)  83.8 us
    dot_general x3, matrix products, coarse_solve(): lax.dot_general(total, coarse_inverse, (((1,), (1,)), ((), ())), precisio...  32.6 us
  transfers between devices with their start and end apart: 19, of which 9 were waited for; matrix products, arithmetic and copies ran while one was open for 0% of the time, Pallas kernels for 0%

commit v1 on v0

--- a/solution.py
+++ b/solution.py
@@ -108,7 +108,7 @@
             - right_link * operate_right_cells
             - left_link * operate_left_cells
         )
-        curvature = lax.psum(jnp.sum(direction * image, axis=(1, 2)), ("str", "crs"))
+        curvature = lax.psum(lax.psum(jnp.sum(direction * image, axis=(1, 2)), "crs"), "str")
         alpha = (product / curvature)[:, None, None]
         newton_step = newton_step + alpha * direction
         remainder = remainder - alpha * image

time: 1070 us -> 1090 us (1.019)
    psum x2 -> x6, blocking collectives: 142 us -> 153 us  [the longest x3 97.1 us: shards(): lax.psum(lax.psum(jnp.sum(direction * image, axis=(1, 2)), 'crs'), 'str')]
where the time goes in v1:
time: 1090 us; the launch traced here: 1070 us
  waiting for transfers between devices  462 us (42%)
  blocking collectives  444 us (41%)
  other arithmetic  50.7 us (5%)
  starting transfers between devices  36.5 us (3%)
  local copies, waits for them, and re-layouts  34.9 us (3%)
  matrix products  32.6 us (3%)
  between operations  14.8 us (1%)
    psum x3, waiting for transfers between devices, coarse_solve(): total = lax.psum(incomplete_value, ('str', 'crs'))  457 us
    psum x3, blocking collectives, precondition(): lax.psum(jnp.sum(remainder * smoothed, axis=(1, 2)), ('str', 'crs'))  207 us
    psum x3, blocking collectives, shards(): lax.psum(lax.psum(jnp.sum(direction * image, axis=(1, 2)), 'crs'), 'str')  97.1 us
    all_gather x3, blocking collectives, coarse_solve(): correction = lax.all_gather(row_share, 'crs', axis=1, tiled=True)  84.1 us
    psum x3, blocking collectives, shards(): lax.psum(jnp.sum(direction * image, axis=(1, 2)), 'crs')  55.5 us
    dot_general x3, matrix products, coarse_solve(): lax.dot_general(total, coarse_inverse, (((1,), (1,)), ((), ())), precisio...  32.6 us
  transfers between devices with their start and end apart: 19, of which 9 were waited for; matrix products, arithmetic and copies ran while one was open for 0% of the time, Pallas kernels for 0%

profile of v1, /device:TPU:1, one launch (start us, length us, event | category | flops | bytes accessed | tf_op | source)
XLA Modules:
  0.0 1074.7 jit_solution(3232352265417213428)
XLA Ops:
  13.7 4.2 collective-permute-start.3
  20.6 2.9 fusion.30
  26.5 3.8 scatter_custom_fusion
  30.4 158.6 %all-reduce.4.cloned.1.call-done = f32[4,4096]{0,1:T(8,128)} async-done(((f32[4,4096]{0,1:T(8,128)}), f32[4,4096]{0,1:T(8,128)}) %all-reduce.4.cloned.1.call-update) | async-done | bytes 65552 | tf_op jit(solution)/shard_map/psum | solution.py:81
  189.0 10.9 %fusion.54 = f32[4,512]{1,0:T(4,128)S(1)} fusion(f32[4,4096]{0,1:T(8,128)} %all-reduce.4.cloned.1.call-done, f32[512,4096]{1,0:T(8,128)} %param.17), kind=kOutput, calls=%fused_computation.118 | convolution fusion | flops 100663296 | bytes 8462336 | tf_op jit(solution)/shard_map/dot_general | solution.py:82
  199.9 28.5 %all_gather.9 = f32[4,4096]{1,0:T(4,128)S(1)} all-gather(f32[4,512]{1,0:T(4,128)S(1)} %fusion.54), channel_id=1, replica_groups=mesh['str'=16,'crs'=8] {'crs'}, dimensions={1}, use_global_device_ids=true | all-gather | bytes 73728 | tf_op jit(solution)/shard_map/all_gather | solution.py:85
  236.1 7.2 collective-permute-start.4
  246.0 4.0 collective-permute-start.7
  252.8 18.1 %psum.86 = f32[4]{0:T(128)} all-reduce(f32[4]{0:T(128)S(1)} %get-tuple-element.3), channel_id=1, replica_groups=mesh['str'=16,'crs'=8] {'crs'}, use_global_device_ids=true, to_apply=%region_6.8 | all-reduce | flops 4 | bytes 32 | tf_op jit(solution)/shard_map/psum | solution.py:111
  271.0 31.5 %psum.87 = f32[4]{0:T(128)} all-reduce(f32[4]{0:T(128)} %psum.86), channel_id=1, replica_groups=mesh['str'=16,'crs'=8] {'str'}, use_global_device_ids=true, to_apply=%region_7.9 | all-reduce | flops 4 | bytes 32 | tf_op jit(solution)/shard_map/psum | solution.py:111
  302.5 66.9 %psum.85 = f32[4]{0:T(128)S(1)} all-reduce(f32[4]{0:T(128)S(1)} %get-tuple-element.4), channel_id=1, replica_groups=mesh['str'=16,'crs'=8] {'str','crs'}, use_global_device_ids=true, to_apply=%region_4.6 | all-reduce | flops 4 | bytes 32 | tf_op jit(solution)/shard_map/psum | solution.py:93
  370.0 2.8 multiply_subtract_fusion.2
  374.7 3.8 scatter_custom_fusion.1
  378.7 147.8 %all-reduce.6.cloned.1.call-done = f32[4,4096]{0,1:T(8,128)} async-done(((f32[4,4096]{0,1:T(8,128)}), f32[4,4096]{0,1:T(8,128)}) %all-reduce.6.cloned.1.call-update) | async-done | bytes 65552 | tf_op jit(solution)/shard_map/psum | solution.py:81
  526.5 10.9 %fusion.55 = f32[4,512]{1,0:T(4,128)S(1)} fusion(f32[4,4096]{0,1:T(8,128)} %all-reduce.6.cloned.1.call-done, f32[512,4096]{1,0:T(8,128)} %param.17), kind=kOutput, calls=%fused_computation.119 | convolution fusion | flops 100663296 | bytes 8462336 | tf_op jit(solution)/shard_map/dot_general | solution.py:82
  537.3 27.8 %all_gather.10 = f32[4,4096]{1,0:T(4,128)S(1)} all-gather(f32[4,512]{1,0:T(4,128)S(1)} %fusion.55), channel_id=1, replica_groups=mesh['str'=16,'crs'=8] {'crs'}, dimensions={1}, use_global_device_ids=true | all-gather | bytes 73728 | tf_op jit(solution)/shard_map/all_gather | solution.py:85
  567.2 3.3 gather_fusion.1
  578.7 69.9 %psum.89 = f32[4]{0:T(128)S(1)} all-reduce(f32[4]{0:T(128)S(1)} %multiply_reduce_fusion.3), channel_id=1, replica_groups=mesh['str'=16,'crs'=8] {'str','crs'}, use_global_device_ids=true, to_apply=%region_12.14 | all-reduce | flops 4 | bytes 32 | tf_op jit(solution)/shard_map/psum | solution.py:93
  653.9 4.0 collective-permute-start.11
  661.2 18.7 %psum.90 = f32[4]{0:T(128)} all-reduce(f32[4]{0:T(128)S(1)} %multiply_reduce_fusion.2), channel_id=1, replica_groups=mesh['str'=16,'crs'=8] {'crs'}, use_global_device_ids=true, to_apply=%region_14.16 | all-reduce | flops 4 | bytes 32 | tf_op jit(solution)/shard_map/psum | solution.py:111
  679.9 32.9 %psum.91 = f32[4]{0:T(128)} all-reduce(f32[4]{0:T(128)} %psum.90), channel_id=1, replica_groups=mesh['str'=16,'crs'=8] {'str'}, use_global_device_ids=true, to_apply=%region_15.17 | all-reduce | flops 4 | bytes 32 | tf_op jit(solution)/shard_map/psum | solution.py:111
  713.5 3.1 multiply_subtract_fusion.1
  721.4 4.1 scatter_custom_fusion.2
  725.5 150.6 %all-reduce.8.cloned.1.call-done = f32[4,4096]{0,1:T(8,128)} async-done(((f32[4,4096]{0,1:T(8,128)}), f32[4,4096]{0,1:T(8,128)}) %all-reduce.8.cloned.1.call-update) | async-done | bytes 65552 | tf_op jit(solution)/shard_map/psum | solution.py:81
  876.1 10.9 %fusion.56 = f32[4,512]{1,0:T(4,128)S(1)} fusion(f32[4,4096]{0,1:T(8,128)} %all-reduce.8.cloned.1.call-done, f32[512,4096]{1,0:T(8,128)} %param.17), kind=kOutput, calls=%fused_computation.120 | convolution fusion | flops 100663296 | bytes 8462336 | tf_op jit(solution)/shard_map/dot_general | solution.py:82
  886.9 27.8 %all_gather.11 = f32[4,4096]{1,0:T(4,128)S(1)} all-gather(f32[4,512]{1,0:T(4,128)S(1)} %fusion.56), channel_id=1, replica_groups=mesh['str'=16,'crs'=8] {'crs'}, dimensions={1}, use_global_device_ids=true | all-gather | bytes 73728 | tf_op jit(solution)/shard_map/all_gather | solution.py:85
  916.7 3.2 gather_fusion.2
  928.5 70.2 %psum.93 = f32[4]{0:T(128)S(1)} all-reduce(f32[4]{0:T(128)S(1)} %multiply_reduce_fusion.1), channel_id=1, replica_groups=mesh['str'=16,'crs'=8] {'str','crs'}, use_global_device_ids=true, to_apply=%region_20.22 | all-reduce | flops 4 | bytes 32 | tf_op jit(solution)/shard_map/psum | solution.py:93
  1003.9 4.0 collective-permute-start.15
  1011.3 18.7 %psum.94 = f32[4]{0:T(128)} all-reduce(f32[4]{0:T(128)S(1)} %multiply_reduce_fusion), channel_id=1, replica_groups=mesh['str'=16,'crs'=8] {'crs'}, use_global_device_ids=true, to_apply=%region_22.24 | all-reduce | flops 4 | bytes 32 | tf_op jit(solution)/shard_map/psum | solution.py:111
  1030.0 32.7 %psum.95 = f32[4]{0:T(128)} all-reduce(f32[4]{0:T(128)} %psum.94), channel_id=1, replica_groups=mesh['str'=16,'crs'=8] {'str'}, use_global_device_ids=true, to_apply=%region_23.25 | all-reduce | flops 4 | bytes 32 | tf_op jit(solution)/shard_map/psum | solution.py:111
  1063.3 2.7 multiply_add_fusion
  (178 shorter events, 73.8 us)
Async XLA Ops:
  7.2 181.8 %all-reduce.4.cloned.1.call-start = ((), (), s32[]{:S(2)}) async-start(), calls=%async_computation | async-start | bytes 4194304 | tf_op jit(solution)/shard_map/psum | solution.py:81
  9.5 10.4 collective-permute-start
  11.0 8.7 collective-permute-start.1
  12.4 7.2 collective-permute-start.2
  13.7 5.9 collective-permute-start.3
  30.3 496.1 %all-reduce.6.cloned.1.call-start = ((), (), s32[]{:S(2)}) async-start(), calls=%async_computation.1 | async-start | bytes 4194304 | tf_op jit(solution)/shard_map/psum | solution.py:81
  199.9 30.8 %copy-start.36 = (pred[512]{0:T(512)(128)(4,1)S(1)}, pred[512]{0:T(512)(128)(4,1)}, u32[]{:S(2)}) copy-start(pred[512]{0:T(512)(128)(4,1)} %compare_and_fusion) | copy-start | bytes 1540
  233.5 18.4 %copy-start.4 = (f32[4,32,2048]{2,1,0:T(8,128)S(1)}, f32[4,32,2048]{2,1,0:T(8,128)}, u32[]{:S(2)}) copy-start(f32[4,32,2048]{2,1,0:T(8,128)} %copy-done.3) | copy-start | bytes 3145732
  233.5 18.4 %copy-start.8 = (f32[32,2048]{1,0:T(8,128)S(1)}, f32[32,2048]{1,0:T(8,128)}, u32[]{:S(2)}) copy-start(f32[32,2048]{1,0:T(8,128)} %copy-done.7) | copy-start | bytes 786436
  233.5 18.4 %copy-start.13 = (f32[32,2048]{1,0:T(8,128)S(1)}, f32[32,2048]{1,0:T(8,128)}, u32[]{:S(2)}) copy-start(f32[32,2048]{1,0:T(8,128)} %copy-done.12) | copy-start | bytes 786436
  233.5 18.4 %copy-start.18 = (f32[32,2048]{1,0:T(8,128)S(1)}, f32[32,2048]{1,0:T(8,128)}, u32[]{:S(2)}) copy-start(f32[32,2048]{1,0:T(8,128)} %copy-done.17) | copy-start | bytes 786436
  236.1 15.7 %collective-permute-start.4 = (f32[4,1,2048]{2,1,0:T(1,128)S(1)}, f32[4,1,2048]{2,1,0:T(1,128)S(1)}, u32[]{:S(2)}, u32[]{:S(2)}) collective-permute-start(f32[4,1,2048]{2,1,0:T(1,128)S(1)} %get-tuple-element.22), channel_id=1, source_target_pairs={{8,0},{16,8},{24,16},{32,24},{40,32},{48,40},{56,48},{64,56},{72,6... | collective-permute-start | bytes 98312 | tf_op jit(solution)/shard_map/ppermute | solution.py:21
  243.3 8.6 collective-permute-start.5
  244.7 5.4 collective-permute-start.6
  246.0 5.9 collective-permute-start.7
  251.9 118.1 %copy-start.5 = (f32[4,32,2048]{2,1,0:T(8,128)S(1)}, f32[4,32,2048]{2,1,0:T(8,128)}, u32[]{:S(2)}) copy-start(f32[4,32,2048]{2,1,0:T(8,128)} %copy-done.3) | copy-start | bytes 3145732
  378.5 497.6 %all-reduce.8.cloned.1.call-start = ((), (), s32[]{:S(2)}) async-start(), calls=%async_computation.2 | async-start | bytes 4194304 | tf_op jit(solution)/shard_map/psum | solution.py:81
  648.7 11.7 %copy-start.9 = (f32[32,2048]{1,0:T(8,128)S(1)}, f32[32,2048]{1,0:T(8,128)}, u32[]{:S(2)}) copy-start(f32[32,2048]{1,0:T(8,128)} %copy-done.7) | copy-start | bytes 786436
  648.7 11.7 %copy-start.14 = (f32[32,2048]{1,0:T(8,128)S(1)}, f32[32,2048]{1,0:T(8,128)}, u32[]{:S(2)}) copy-start(f32[32,2048]{1,0:T(8,128)} %copy-done.12) | copy-start | bytes 786436
  648.7 11.7 %copy-start.19 = (f32[32,2048]{1,0:T(8,128)S(1)}, f32[32,2048]{1,0:T(8,128)}, u32[]{:S(2)}) copy-start(f32[32,2048]{1,0:T(8,128)} %copy-done.17) | copy-start | bytes 786436
  650.7 8.5 collective-permute-start.8
  651.9 7.3 collective-permute-start.9
  652.6 5.7 collective-permute-start.10
  653.9 5.3 collective-permute-start.11
  926.7 72.1 %copy-start.41 = (f32[4]{0:T(128)S(1)}, f32[4]{0:T(128)}, u32[]{:S(2)}) copy-start(f32[4]{0:T(128)} %copy-done.40) | copy-start | bytes 52
  998.7 11.7 %copy-start.10 = (f32[32,2048]{1,0:T(8,128)S(1)}, f32[32,2048]{1,0:T(8,128)}, u32[]{:S(2)}) copy-start(f32[32,2048]{1,0:T(8,128)} %copy-done.7) | copy-start | bytes 786436
  998.8 11.7 %copy-start.15 = (f32[32,2048]{1,0:T(8,128)S(1)}, f32[32,2048]{1,0:T(8,128)}, u32[]{:S(2)}) copy-start(f32[32,2048]{1,0:T(8,128)} %copy-done.12) | copy-start | bytes 786436
  998.8 11.7 %copy-start.20 = (f32[32,2048]{1,0:T(8,128)S(1)}, f32[32,2048]{1,0:T(8,128)}, u32[]{:S(2)}) copy-start(f32[32,2048]{1,0:T(8,128)} %copy-done.17) | copy-start | bytes 786436
  1000.8 8.5 collective-permute-start.12
  1001.9 7.3 collective-permute-start.13
  1002.7 5.7 collective-permute-start.14
  1003.9 5.3 collective-permute-start.15
  (29 other events, 98.5 us)
Sparse Core Ops, SparseCore 0:
  30.5 158.5 all-reduce.3
  378.6 147.8 all-reduce.5
  725.6 150.4 all-reduce.7
